TPU v7x, 512 devices: a whole 4x8x8 slice. The times are simulated.
512 devices in a mesh: aa: 32 (over y_lo, z, core), ba: 16 (over x, y_hi).
Axes of the slice: x: 4, y: 8 (y_hi: 4, y_lo: 2; y = y_hi * 2 + y_lo), z: 8, core: 2. Of those that a mesh axis runs over, the one named last changes fastest.
Arguments:
- frame_one: bfloat16 [32768, 128], P('aa'), may hold values from -40 to 40
- frame_two: bfloat16 [32768, 128], P('ba'), may hold values from -40 to 40
Outputs:
- warped_one: float32 [32768, 128], P(('aa', 'ba'))
- flow_one: float32 [2, 32768], P(None, ('aa', 'ba'))
- warped_two: float32 [32768, 128], P(('ba', 'aa'))
- flow_two: float32 [2, 32768], P(None, ('ba', 'aa'))
All inputs are finite; a program needn't handle non-finite values.
Results may differ from a plain program's by a relative error of at most 0.0039.
Values sent between devices are 32-bit elements; how exact they have to be, the bound alone decides.
A program may use at most 64 MiB of HBM per device.

v0:
```python
import jax
import jax.numpy as jnp
from jax import lax
from jax.sharding import PartitionSpec as P

IMG_W = 128


def pixel_grid(start_pos, total_rows):
    position = start_pos + jnp.arange(total_rows, dtype=jnp.int32)
    column_pos = (position % IMG_W).astype(jnp.float32) / 64.0
    row_pos = (position // IMG_W).astype(jnp.float32) / 64.0
    return jnp.stack([column_pos, row_pos]).astype(jnp.bfloat16)


def shards(frame_one, frame_two):
    rows_one, channels = frame_one.shape
    rows_two = frame_two.shape[0]
    factor = channels ** (-0.5)
    block_rows = 256
    block_count = rows_one // block_rows
    grid_one = pixel_grid(lax.axis_index("aa") * rows_one, rows_one)
    grid_two = pixel_grid(lax.axis_index("ba") * rows_two, rows_two)
    tiles = frame_one.reshape(block_count, block_rows, channels)
    grid_tiles = grid_one.reshape(2, block_count, block_rows).transpose(1, 0, 2)

    def scores(tile_rows):
        return (
            lax.dot_general(
                tile_rows, frame_two, (((1,), (1,)), ((), ())), preferred_element_type=jnp.float32
            )
            * factor
        )

    def peak_pass(state_peak, tile_rows):
        scores_now = scores(tile_rows)
        return (jnp.maximum(state_peak, scores_now.max(axis=0)), scores_now.max(axis=1))

    local_peak, local_rows = lax.scan(
        peak_pass, jnp.full((rows_two,), -jnp.inf, jnp.float32), tiles
    )
    row_peaks = lax.pmax(local_rows.reshape(-1), "ba")
    col_peak = lax.pmax(local_peak, "aa")

    def total_pass(state_total, inputs):
        tile_rows, row_peak = inputs
        scores_now = scores(tile_rows)
        column_part = jnp.exp(scores_now - col_peak[None, :]).sum(axis=0)
        return (state_total + column_part, jnp.exp(scores_now - row_peak[:, None]).sum(axis=1))

    local_total, local_rows = lax.scan(
        total_pass,
        jnp.zeros((rows_two,), jnp.float32),
        (tiles, row_peaks.reshape(block_count, block_rows)),
    )
    row_totals = lax.psum(local_rows.reshape(-1), "ba")
    col_total = lax.psum(local_total, "aa")

    def second_pass(state_pair, inputs):
        tile_rows, tile_grid, row_peak, row_total = inputs
        scores_now = scores(tile_rows)
        forward = (jnp.exp(scores_now - row_peak[:, None]) / row_total[:, None]).astype(
            jnp.bfloat16
        )
        backward = (jnp.exp(scores_now - col_peak[None, :]) / col_total[None, :]).astype(
            jnp.bfloat16
        )
        forward_feat = jnp.dot(forward, frame_two, preferred_element_type=jnp.float32)
        forward_coord = lax.dot_general(
            grid_two, forward, (((1,), (1,)), ((), ())), preferred_element_type=jnp.float32
        )
        back_feat = state_pair[0] + lax.dot_general(
            backward, tile_rows, (((0,), (0,)), ((), ())), preferred_element_type=jnp.float32
        )
        back_coord = state_pair[1] + jnp.dot(
            tile_grid, backward, preferred_element_type=jnp.float32
        )
        return ((back_feat, back_coord), (forward_feat, forward_coord))

    start_back = (
        jnp.zeros((rows_two, channels), jnp.float32),
        jnp.zeros((2, rows_two), jnp.float32),
    )
    (back_feat, back_coord), (forward_feat, forward_coord) = lax.scan(
        second_pass,
        start_back,
        (
            tiles,
            grid_tiles,
            row_peaks.reshape(block_count, block_rows),
            row_totals.reshape(block_count, block_rows),
        ),
    )
    forward_feat = forward_feat.reshape(rows_one, channels)
    forward_coord = forward_coord.transpose(1, 0, 2).reshape(2, rows_one)
    share_one = rows_one // lax.axis_size("ba")
    offset_one = lax.axis_index("ba") * share_one
    share_two = rows_two // lax.axis_size("aa")
    offset_two = lax.axis_index("aa") * share_two
    forward_feat, forward_coord = lax.psum((forward_feat, forward_coord), "ba")
    forward_feat = lax.dynamic_slice_in_dim(forward_feat, offset_one, share_one, 0)
    forward_coord = lax.dynamic_slice_in_dim(forward_coord, offset_one, share_one, 1)
    back_feat, back_coord = lax.psum((back_feat, back_coord), "aa")
    back_feat = lax.dynamic_slice_in_dim(back_feat, offset_two, share_two, 0)
    back_coord = lax.dynamic_slice_in_dim(back_coord, offset_two, share_two, 1)
    own_one = lax.dynamic_slice_in_dim(grid_one, offset_one, share_one, 1).astype(jnp.float32)
    own_two = lax.dynamic_slice_in_dim(grid_two, offset_two, share_two, 1).astype(jnp.float32)
    flow_one = forward_coord - own_one
    flow_two = back_coord - own_two
    return (forward_feat, flow_one, back_feat, flow_two)


def solution(mesh):
    return jax.shard_map(
        shards,
        mesh=mesh,
        in_specs=(P("aa", None), P("ba", None)),
        out_specs=(
            P(("aa", "ba"), None),
            P(None, ("aa", "ba")),
            P(("ba", "aa"), None),
            P(None, ("ba", "aa")),
        ),
        check_vma=False,
    )
```

profile of v0, /device:TPU:1, one launch (start us, length us, event | category | flops | bytes accessed | tf_op | source)
XLA Modules:
  0.0 649.0 jit_solution(2696202758178914253)
XLA Ops:
  7.3 6.7 %while.43 = (s32[]{:T(128)}, f32[2048]{0:T(1024)S(1)}, f32[4,256]{1,0:T(4,128)S(1)}, bf16[4,256,128]{2,1,0:T(8,128)(2,1)}, bf16[2048,128]{1,0:T(8,128)(2,1)}, /*index=5*/s32[]{:T(128)}, s32[]{:T(128)}) while((s32[]{:T(128)}, f32[2048]{0:T(1024)S(1)}, f32[4,256]{1,0:T(4,128)S(1)}, bf16[4,256,128]{2,1,0:T(8,128)(2,1)}, ...), condition=%wide.region_3.4_spmd.clone, body=%wide.region_0.3_spmd.clone.sunk | while | flops 135792384 | bytes 625767 | solution.py:39
  10.6 1.6 fusion.54
  14.0 39.1 %pmax.15 = f32[4,256]{1,0:T(4,128)S(1)} all-reduce(f32[4,256]{1,0:T(4,128)S(1)} %get-tuple-element.141), channel_id=1, replica_groups=mesh['aa'=32,'ba'=16] {'ba'}, use_global_device_ids=true, to_apply=%region_4.5 | all-reduce | flops 1024 | bytes 8192 | tf_op jit(solution)/shard_map/pmax | solution.py:42
  53.1 66.7 %pmax.14 = f32[2048]{0:T(1024)S(1)} all-reduce(f32[2048]{0:T(1024)S(1)} %get-tuple-element.140), channel_id=1, replica_groups=mesh['aa'=32,'ba'=16] {'aa'}, use_global_device_ids=true, to_apply=%region_5.6 | all-reduce | flops 2048 | bytes 16384 | tf_op jit(solution)/shard_map/pmax | solution.py:43
  119.8 8.3 %while.44 = (s32[]{:T(128)}, f32[2048]{0:T(1024)S(1)}, f32[4,256]{1,0:T(4,128)S(1)}, bf16[4,256,128]{2,1,0:T(8,128)(2,1)}, bf16[2048,128]{1,0:T(8,128)(2,1)}, /*...) while((s32[]{:T(128)}, f32[2048]{0:T(1024)S(1)}, f32[4,256]{1,0:T(4,128)S(1)}, ...), condition=%wide.region_9.10_spmd.clone, body=%wide.region_6.9_spmd.clone.sunk | while | flops 136840960 | bytes 637051 | solution.py:51
  119.8 2.0 exponential_reduce_fusion.3
  121.8 2.0 exponential_reduce_fusion.3
  123.9 2.0 exponential_reduce_fusion.3
  126.0 2.0 exponential_reduce_fusion.3
  128.0 32.1 %psum.43 = f32[4,256]{1,0:T(4,128)S(1)} all-reduce(f32[4,256]{1,0:T(4,128)S(1)} %get-tuple-element.143), channel_id=1, replica_groups=mesh['aa'=32,'ba'=16] {'ba'}, use_global_device_ids=true, to_apply=%region_10.11 | all-reduce | flops 1024 | bytes 8192 | tf_op jit(solution)/shard_map/psum | solution.py:56
  160.1 60.4 %psum.42 = f32[2048]{0:T(1024)S(1)} all-reduce(f32[2048]{0:T(1024)S(1)} %get-tuple-element.142), channel_id=1, replica_groups=mesh['aa'=32,'ba'=16] {'aa'}, use_global_device_ids=true, to_apply=%region_11.12 | all-reduce | flops 2048 | bytes 16384 | tf_op jit(solution)/shard_map/psum | solution.py:57
  220.8 24.6 %while.45 = (s32[]{:T(128)}, f32[2048,128]{1,0:T(8,128)S(1)}, f32[2,2048]{1,0:T(2,128)S(1)}, f32[4,256,128]{2,1,0:T(8,128)}, f32[4,2,256]{2,1,0:T(2,128)S(1)}, /...) while((s32[]{:T(128)}, f32[2048,128]{1,0:T(8,128)S(1)}, ...), condition=%wide.region_13.14_spmd.clone, body=%wide.region_12.13_spmd.clone.sunk | while | flops 411049984 | bytes 11863252 | solution.py:84
  220.8 2.0 divide_convert_fusion.3
  225.2 1.7 convolution_add_fusion.4
  227.0 2.0 divide_convert_fusion.3
  231.3 1.7 convolution_add_fusion.4
  233.1 2.0 divide_convert_fusion.3
  237.5 1.7 convolution_add_fusion.4
  239.3 2.0 divide_convert_fusion.3
  243.6 1.7 convolution_add_fusion.4
  246.4 36.1 %psum.45 = f32[2,1024]{1,0:T(2,128)S(1)} all-reduce(f32[2,1024]{1,0:T(2,128)S(1)} %bitcast.100), channel_id=1, replica_groups=mesh['aa'=32,'ba'=16] {'ba'}, use_global_device_ids=true, to_apply=%region_15.16 | all-reduce | flops 2048 | bytes 16384 | tf_op jit(solution)/shard_map/psum | solution.py:100
  282.5 111.5 %psum.47 = f32[2,2048]{1,0:T(2,128)S(1)} all-reduce(f32[2,2048]{1,0:T(2,128)S(1)} %get-tuple-element.147), channel_id=1, replica_groups=mesh['aa'=32,'ba'=16] {'aa'}, use_global_device_ids=true, to_apply=%region_17.18 | all-reduce | flops 4096 | bytes 32768 | tf_op jit(solution)/shard_map/psum | solution.py:103
  395.3 4.1 all-reduce.3.cloned.1.call-done
  400.8 240.0 %all-reduce.5.cloned.1.call-done = f32[2048,128]{1,0:T(8,128)} async-done(((f32[2048,128]{1,0:T(8,128)}), f32[2048,128]{1,0:T(8,128)}) %all-reduce.5.cloned.1.call-update) | async-done | bytes 1048592 | tf_op jit(solution)/shard_map/psum | solution.py:103
  (70 shorter events, 20.0 us)
Async XLA Ops:
  7.2 392.2 %all-reduce.3.cloned.1.call-start = ((), (), s32[]{:S(2)}) async-start(), calls=%async_computation | async-start | bytes 1048576 | tf_op jit(solution)/shard_map/psum | solution.py:100
  222.8 1.0 copy-start.1
  229.0 1.0 copy-start.1
  235.1 1.0 copy-start.1
  241.2 1.0 copy-start.1
  245.4 1.0 copy-start
  245.4 395.4 %all-reduce.5.cloned.1.call-start = ((), (), s32[]{:S(2)}) async-start(), calls=%async_computation.1 | async-start | bytes 2097152 | tf_op jit(solution)/shard_map/psum | solution.py:103
Sparse Core Ops, SparseCore 0:
  245.5 153.8 all-reduce.2
  402.6 238.1 all-reduce.4
where the time goes:
time: 650 us; the launch traced here: 649 us
  blocking collectives  346 us (53%)
  waiting for transfers between devices  244 us (38%)
  matrix products  36.1 us (6%)
  between operations  14.2 us (2%)
  local copies, waits for them, and re-layouts  6.69 us (1%)
    psum x1, waiting for transfers between devices, shards(): back_feat, back_coord = lax.psum((back_feat, back_coord), 'aa')  240 us
    psum x1, blocking collectives, shards(): back_feat, back_coord = lax.psum((back_feat, back_coord), 'aa')  111 us
    pmax x1, blocking collectives, shards(): col_peak = lax.pmax(local_peak, 'aa')  66.7 us
    psum x1, blocking collectives, shards(): col_total = lax.psum(local_total, 'aa')  60.4 us
    pmax x1, blocking collectives, shards(): row_peaks = lax.pmax(local_rows.reshape(-1), 'ba')  39.1 us
    psum x1, blocking collectives, shards(): forward_feat, forward_coord = lax.psum((forward_feat, forward_coord), 'ba')  36.1 us
    psum x1, blocking collectives, shards(): row_totals = lax.psum(local_rows.reshape(-1), 'ba')  32.1 us
    dot_general x12, matrix products, scores(): lax.dot_general(tile_rows, frame_two, (((1,), (1,)), ((), ())), preferred...  22.3 us
  transfers between devices with their start and end apart: 2, of which 2 were waited for; matrix products, arithmetic and copies ran while one was open for 0% of the time, Pallas kernels for 0%

commit v1 on v0

v1 whole, which is shorter than its diff:
```python
import functools
import math

import jax
import jax.numpy as jnp
from jax import lax
from jax.experimental import pallas as pl
from jax.experimental.pallas import tpu as pltpu
from jax.sharding import PartitionSpec as P

IMG_W = 128
CH = 128
MSG = CH + 8
AUG = CH + 16
CHUNK = 256
PART = 64
PACK = PART + 8
SCALE = CH ** (-0.5) * math.log2(math.e)
MESH = pl.DeviceIdType.MESH
F32 = jnp.float32
BF16 = jnp.bfloat16


def grid_xy(pixel):
    column_pos = lax.rem(pixel, IMG_W).astype(F32) / 64.0
    row_pos = lax.div(pixel, IMG_W).astype(F32) / 64.0
    return column_pos, row_pos


def put_keys(kt, start, keys, first_pixel):
    count = keys.shape[0]
    cols = pl.ds(start, count)
    kt[0:CH, cols] = keys.T
    row = lax.broadcasted_iota(jnp.int32, (16, count), 0)
    pixel = first_pixel + lax.broadcasted_iota(jnp.int32, (16, count), 1)
    column_pos, row_pos = grid_xy(pixel)
    extra = jnp.where(row == 0, column_pos, jnp.where(row == 1, row_pos, jnp.where(row == 2, 1.0, 0.0)))
    kt[CH:AUG, cols] = extra.astype(BF16)


def attend(queries, keys, kt, scores):
    count = keys.shape[0]
    scores[0:count, :] = lax.dot_general(
        keys, queries, (((1,), (1,)), ((), ())), preferred_element_type=F32
    )
    peak = jnp.max(scores[0:count, :], axis=0, keepdims=True)
    weights = jnp.exp2((scores[0:count, :] - peak) * SCALE).astype(BF16)
    total = jnp.dot(kt, weights, preferred_element_type=F32)
    row = lax.broadcasted_iota(jnp.int32, (8, CHUNK), 0)
    return total[0:CH], jnp.where(row == 3, peak, total[CH:MSG])


def merge(parts):
    peaks = [extra[3:4] for _, extra in parts]
    peak = functools.reduce(jnp.maximum, peaks)
    gains = [jnp.exp2((p - peak) * SCALE) for p in peaks]
    feat = sum(f * g for (f, _), g in zip(parts, gains))
    extra = sum(e * g for (_, e), g in zip(parts, gains))
    row = lax.broadcasted_iota(jnp.int32, extra.shape, 0)
    return feat, jnp.where(row == 3, peak, extra)


def pack(feat, extra, out):
    low_lane = lax.broadcasted_iota(jnp.int32, (PART, CH), 1) < PART
    low_extra = lax.broadcasted_iota(jnp.int32, (8, CH), 1) < PART
    for t in range(2):
        low, high = feat[0:PART, t * CH:(t + 1) * CH], feat[PART:CH, t * CH:(t + 1) * CH]
        ext = extra[:, t * CH:(t + 1) * CH]
        ext_roll = pltpu.roll(ext, PART, 1)
        out[2 * t, 0:PART] = jnp.where(low_lane, low, pltpu.roll(high, PART, 1))
        out[2 * t, PART:PACK] = jnp.where(low_extra, ext, ext_roll)
        out[2 * t + 1, 0:PART] = jnp.where(low_lane, pltpu.roll(low, PART, 1), high)
        out[2 * t + 1, PART:PACK] = jnp.where(low_extra, ext_roll, ext)


def finish(parts, first_pixel, warped, flow):
    feat, extra = merge(parts)
    inverse = 1.0 / extra[2:3]
    turned = (feat * inverse).T
    warped[:, 0:PART] = turned[0:PART]
    warped[:, PART:CH] = turned[PART:CH]
    pixel = first_pixel + lax.broadcasted_iota(jnp.int32, (1, PART), 1)
    column_pos, row_pos = grid_xy(pixel)
    coord = (extra * inverse)[:, 0:PART]
    flow[0:1] = coord[0:1] - column_pos
    flow[1:2] = coord[1:2] - row_pos


def kernel(
    f1, f2, warped_one, flow_one, warped_two, flow_two,
    sent_keys, got_keys, keys_one, kt_one, kt_two, scores,
    a1_out, a1_in, b1_out, b1_in, a2_out, a2_in, b2_out, b2_in,
    core_send, core_recv, a1_send, a1_recv, b1_send, b1_recv,
    a2_send, a2_recv, b2_send, b2_recv,
):
    aa, ba = lax.axis_index("aa"), lax.axis_index("ba")
    core = lax.rem(aa, 2)
    z = lax.rem(lax.div(aa, 2), 8)
    y_lo = lax.div(aa, 16)
    z_hi, z_lo = lax.div(z, 2), lax.rem(z, 2)
    x, y_hi = lax.div(ba, 4), lax.rem(ba, 4)
    group = y_lo * 2 + z_lo
    rows_one = f1.shape[0]

    def turn(value, offset):
        return lax.rem(value + offset, 4)

    def a1_peer(offset):
        return (aa, turn(x, offset) * 4 + y_hi)

    def a2_peer(offset):
        return (aa, x * 4 + turn(y_hi, offset))

    def b1_peer(offset):
        to = turn(group, offset)
        return ((lax.div(to, 2) * 8 + z_hi * 2 + lax.rem(to, 2)) * 2 + core, ba)

    def b2_peer(offset):
        return ((y_lo * 8 + turn(z_hi, offset) * 2 + z_lo) * 2 + core, ba)

    sibling = (aa + 1 - 2 * core, ba)

    def remote(src, dst, send, recv, peer):
        return pltpu.make_async_remote_copy(
            src_ref=src, dst_ref=dst, send_sem=send, recv_sem=recv, device_id=peer, device_id_type=MESH
        )

    def a1_copy(s):
        return remote(a1_out.at[s], a1_in.at[s], a1_send.at[s], a1_recv.at[s], a1_peer(s + 1))

    def b1_copy(s):
        return remote(b1_out.at[s], b1_in.at[s], b1_send.at[s], b1_recv.at[s], b1_peer(s + 1))

    def a2_copy(s):
        return remote(
            a2_out.at[turn(y_hi, s + 1)], a2_in.at[s], a2_send.at[s], a2_recv.at[s], a2_peer(s + 1)
        )

    def b2_copy(s):
        return remote(
            b2_out.at[turn(z_hi, s + 1)], b2_in.at[s], b2_send.at[s], b2_recv.at[s], b2_peer(s + 1)
        )

    barrier = pltpu.get_barrier_semaphore()
    for peers in (a1_peer, a2_peer, b1_peer, b2_peer):
        for s in range(3):
            pl.semaphore_signal(barrier, inc=1, device_id=peers(s + 1), device_id_type=MESH)
    pl.semaphore_signal(barrier, inc=1, device_id=sibling, device_id_type=MESH)

    sent_keys[...] = f1[...].astype(F32)
    put_keys(kt_two, 0, f2[...], ba * f2.shape[0])

    def a_chunk(s):
        start = pl.multiple_of(turn(x, s + 1) * CHUNK, CHUNK)
        feat, extra = attend(f1[pl.ds(start, CHUNK)], f2[...], kt_two[...], scores)
        a1_out[s, 0:CH] = feat
        a1_out[s, CH:MSG] = extra

    def b_queries(s):
        to = turn(group, s + 1)
        first = lax.div(to, 2) * 8 + lax.rem(to, 2)
        blocks = []
        for j in range(4):
            start = pl.multiple_of(((first + 2 * j) * 2 + core) * PART, PART)
            blocks.append(f2[pl.ds(start, PART)])
        return jnp.concatenate(blocks, axis=0)

    def a_early(s, carry):
        a_chunk(s)
        return carry

    lax.fori_loop(0, 2, a_early, 0)
    pl.semaphore_wait(barrier, 13)
    keys_copy = remote(sent_keys, got_keys, core_send, core_recv, sibling)
    keys_copy.start()
    a1_copy(0).start()
    a1_copy(1).start()

    def a_late(s, carry):
        a_chunk(s)

        @pl.when(s < 3)
        def _():
            a1_copy(s).start()

        return carry

    lax.fori_loop(2, 4, a_late, 0)

    put_keys(kt_one, 0, f1[...], aa * rows_one)

    def b_early(s, carry):
        feat, extra = attend(b_queries(s), f1[...], kt_one[:, 0:rows_one], scores)
        b1_out[s, 0:CH] = feat
        b1_out[s, CH:MSG] = extra
        return carry

    lax.fori_loop(0, 4, b_early, 0)

    keys_copy.wait_recv()
    keys_one[...] = got_keys[...].astype(BF16)
    put_keys(kt_one, rows_one, keys_one[...], sibling[0] * rows_one)

    def b_late(s, carry):
        part = attend(
            b_queries(s), keys_one[...], kt_one[:, rows_one:2 * rows_one], scores
        )
        feat, extra = merge([(b1_out[s, 0:CH], b1_out[s, CH:MSG]), part])
        b1_out[s, 0:CH] = feat
        b1_out[s, CH:MSG] = extra

        @pl.when(s < 3)
        def _():
            b1_copy(s).start()

        return carry

    lax.fori_loop(0, 4, b_late, 0)

    def first_merge(own, got, out):
        parts = [(own[3, 0:CH], own[3, CH:MSG])]
        parts += [(got[s, 0:CH], got[s, CH:MSG]) for s in range(3)]
        feat, extra = merge(parts)
        pack(feat, extra, out)

    def last_merge(mine, out, got, first_pixel, warped, flow):
        parts = [(out[mine, 0:PART], out[mine, PART:PACK])]
        parts += [(got[s, 0:PART], got[s, PART:PACK]) for s in range(3)]
        finish(parts, first_pixel, warped, flow)

    for s in range(3):
        a1_copy(s).wait_recv()
    first_merge(a1_out, a1_in, a2_out)
    for s in range(3):
        a2_copy(s).start()
    for s in range(3):
        b1_copy(s).wait_recv()
    first_merge(b1_out, b1_in, b2_out)
    for s in range(3):
        b2_copy(s).start()
    for s in range(3):
        a2_copy(s).wait_recv()
    last_merge(y_hi, a2_out, a2_in, (aa * 16 + ba) * PART, warped_one, flow_one)
    for s in range(3):
        b2_copy(s).wait_recv()
    last_merge(z_hi, b2_out, b2_in, (ba * 32 + aa) * PART, warped_two, flow_two)

    keys_copy.wait_send()
    for s in range(3):
        a1_copy(s).wait_send()
        b1_copy(s).wait_send()
        a2_copy(s).wait_send()
        b2_copy(s).wait_send()


def shards(frame_one, frame_two):
    rows_one, rows_two = frame_one.shape[0], frame_two.shape[0]
    vmem = pl.BlockSpec(memory_space=pltpu.VMEM)
    dma = pltpu.SemaphoreType.DMA
    return pl.pallas_call(
        kernel,
        out_shape=(
            jax.ShapeDtypeStruct((PART, CH), F32),
            jax.ShapeDtypeStruct((2, PART), F32),
            jax.ShapeDtypeStruct((PART, CH), F32),
            jax.ShapeDtypeStruct((2, PART), F32),
        ),
        in_specs=[vmem, vmem],
        out_specs=(vmem,) * 4,
        scratch_shapes=[
            pltpu.VMEM((rows_one, CH), F32),
            pltpu.VMEM((rows_one, CH), F32),
            pltpu.VMEM((rows_one, CH), BF16),
            pltpu.VMEM((AUG, 2 * rows_one), BF16),
            pltpu.VMEM((AUG, rows_two), BF16),
            pltpu.VMEM((rows_two, CHUNK), F32),
            pltpu.VMEM((4, MSG, CHUNK), F32),
            pltpu.VMEM((3, MSG, CHUNK), F32),
            pltpu.VMEM((4, MSG, CHUNK), F32),
            pltpu.VMEM((3, MSG, CHUNK), F32),
            pltpu.VMEM((4, PACK, CH), F32),
            pltpu.VMEM((3, PACK, CH), F32),
            pltpu.VMEM((4, PACK, CH), F32),
            pltpu.VMEM((3, PACK, CH), F32),
            dma, dma,
            dma((3,)), dma((3,)), dma((3,)), dma((3,)),
            dma((3,)), dma((3,)), dma((3,)), dma((3,)),
        ],
        compiler_params=pltpu.CompilerParams(
            collective_id=0, has_side_effects=True, vmem_limit_bytes=40 * 1024 * 1024
        ),
        name="match",
    )(frame_one, frame_two)


def solution(mesh):
    return jax.shard_map(
        shards,
        mesh=mesh,
        in_specs=(P("aa", None), P("ba", None)),
        out_specs=(
            P(("aa", "ba"), None),
            P(None, ("aa", "ba")),
            P(("ba", "aa"), None),
            P(None, ("ba", "aa")),
        ),
        check_vma=False,
    )
```

time: 650 us -> 39.3 us (0.06)
  blocking collectives: 346 us -> 0 us
  waiting for transfers between devices: 244 us -> 0 us
  matrix products: 36.1 us -> 0 us
  Pallas kernels: 0 us -> 34.1 us
  between operations: 14.2 us -> 0.65 us
    psum x2 -> x0, waiting for transfers between devices: 244 us -> none  [the longest x1 240 us: shards(): back_feat, back_coord = lax.psum((back_feat, back_coord), 'aa')]
    psum x4 -> x0, blocking collectives: 240 us -> none  [the longest x1 111 us: shards(): back_feat, back_coord = lax.psum((back_feat, back_coord), 'aa')]
    pmax x2 -> x0, blocking collectives: 106 us -> none  [the longest x1 66.7 us: shards(): col_peak = lax.pmax(local_peak, 'aa')]
    dot_general x28 -> x0, matrix products: 36.1 us -> none  [the longest x12 22.3 us: scores(): lax.dot_general(tile_rows, frame_two, (((1,), (1,)), ((), ())), preferred...]
    pallas_call x0 -> x1, Pallas kernels: none -> 34.1 us  [shards(): pl.pallas_call(kernel, out_shape=(jax.ShapeDtypeStruct((PART, CH), F32),...]
  transfers between devices with their start and end apart: 2 -> 0, of which waited for: 2 -> 0; matrix products, arithmetic and copies ran while one was open for 0% -> 0% of each run, Pallas kernels for 0% -> 0%
where the time goes in v1:
time: 39.3 us; the launch traced here: 39.1 us
  Pallas kernels  34.1 us (87%)
  local copies, waits for them, and re-layouts  4.34 us (11%)
  between operations  0.65 us (2%)
    pallas_call x1, Pallas kernels, shards(): pl.pallas_call(kernel, out_shape=(jax.ShapeDtypeStruct((PART, CH), F32),...  34.1 us
    unnamed x8, local copies, waits for them, and re-layouts  4.34 us

profile of v1, /device:TPU:1, one launch (start us, length us, event | category | flops | bytes accessed | tf_op | source)
XLA Modules:
  0.0 39.1 jit_solution(3610087375961070576)
XLA Ops:
  0.6 0.0 copy-start
  0.6 1.0 %copy-done = bf16[2048,128]{1,0:T(8,128)(2,1)S(1)} copy-done((bf16[2048,128]{1,0:T(8,128)(2,1)S(1)}, bf16[2048,128]{1,0:T(8,128)(2,1)}, u32[]{:S(2)}) %copy-start) | copy-done | bytes 524312
  1.7 0.0 copy-start.1
  1.7 0.9 %copy-done.1 = bf16[1024,128]{1,0:T(8,128)(2,1)S(1)} copy-done((bf16[1024,128]{1,0:T(8,128)(2,1)S(1)}, bf16[1024,128]{1,0:T(8,128)(2,1)}, u32[]{:S(2)}) %copy-start.1) | copy-done | bytes 262168
  2.6 34.1 %match.1 = (f32[64,128]{1,0:T(8,128)S(1)}, f32[2,64]{1,0:T(2,128)S(1)}, f32[64,128]{1,0:T(8,128)S(1)}, f32[2,64]{1,0:T(2,128)S(1)}) custom-call(bf16[1024,128]{1,0:T(8,128)(2,1)S(1)} %copy-done.1, bf16[2048,128]{1,0:T(8,128)(2,1)S(1)} %copy-done), custom_call_target="tpu_custom_call" | custom-call | tf_op jit(solution)/shard_map/match/pallas_call | solution.py:260
  36.8 0.6 %copy.10 = f32[64,128]{1,0:T(8,128)} copy(f32[64,128]{1,0:T(8,128)S(1)} %get-tuple-element.8) | data formatting | bytes 65536
  37.4 0.6 %copy.11 = f32[2,64]{1,0:T(2,128)} copy(f32[2,64]{1,0:T(2,128)S(1)} %get-tuple-element.9) | data formatting | bytes 1024
  37.9 0.6 %copy.12 = f32[64,128]{1,0:T(8,128)} copy(f32[64,128]{1,0:T(8,128)S(1)} %get-tuple-element.10) | data formatting | bytes 65536
  38.5 0.6 %copy.13 = f32[2,64]{1,0:T(2,128)} copy(f32[2,64]{1,0:T(2,128)S(1)} %get-tuple-element.11) | data formatting | bytes 1024
Async XLA Ops:
  0.6 1.0 %copy-start = (bf16[2048,128]{1,0:T(8,128)(2,1)S(1)}, bf16[2048,128]{1,0:T(8,128)(2,1)}, u32[]{:S(2)}) copy-start(bf16[2048,128]{1,0:T(8,128)(2,1)} %f2.1) | copy-start | bytes 1572868
  1.7 0.9 %copy-start.1 = (bf16[1024,128]{1,0:T(8,128)(2,1)S(1)}, bf16[1024,128]{1,0:T(8,128)(2,1)}, u32[]{:S(2)}) copy-start(bf16[1024,128]{1,0:T(8,128)(2,1)} %f1.1) | copy-start | bytes 786436

commit v2 on v1

v2 whole, which is shorter than its diff:
```python
import functools
import math

import jax
import jax.numpy as jnp
from jax import lax
from jax.experimental import pallas as pl
from jax.experimental.pallas import tpu as pltpu
from jax.sharding import PartitionSpec as P

IMG_W = 128
CH = 128
MSG = CH + 8
AUG = CH + 16
CHUNK = 256
PART = 64
PACK = PART + 8
TILE = 512
SCALE = CH ** (-0.5) * math.log2(math.e)
MESH = pl.DeviceIdType.MESH
A_ORDER = (2, 1, 3, 0)
B_ORDER = (3, 2, 1, 0)
F32 = jnp.float32
BF16 = jnp.bfloat16


def grid_xy(pixel):
    column_pos = lax.rem(pixel, IMG_W).astype(F32) / 64.0
    row_pos = lax.div(pixel, IMG_W).astype(F32) / 64.0
    return column_pos, row_pos


def put_keys(kt, start, keys, first_pixel):
    count = keys.shape[0]
    cols = pl.ds(start, count)
    kt[0:CH, cols] = keys.T
    row = lax.broadcasted_iota(jnp.int32, (16, count), 0)
    pixel = first_pixel + lax.broadcasted_iota(jnp.int32, (16, count), 1)
    column_pos, row_pos = grid_xy(pixel)
    extra = jnp.where(row == 0, column_pos, jnp.where(row == 1, row_pos, jnp.where(row == 2, 1.0, 0.0)))
    kt[CH:AUG, cols] = extra.astype(BF16)


def score_steps(queries, keys, scores, peaks):
    def step(first):
        rows = slice(first, first + TILE)
        tile = lax.dot_general(
            keys[rows], queries, (((1,), (1,)), ((), ())), preferred_element_type=F32
        )
        scores[rows] = tile
        peaks.append(jnp.max(tile.reshape(TILE // 8, 8, CHUNK), axis=0))

    return [functools.partial(step, first) for first in range(0, keys.shape[0], TILE)]


def sum_steps(kt, scores, peak, sums):
    def step(first):
        cols = slice(first, first + TILE)
        weights = jnp.exp2((scores[cols] - peak) * SCALE).astype(BF16)
        sums.append(jnp.dot(kt[:, cols], weights, preferred_element_type=F32))

    return [functools.partial(step, first) for first in range(0, kt.shape[1], TILE)]


def attend(units, scores):
    peaks = []
    for step in score_steps(units[0][0](), units[0][1], scores[0], peaks):
        step()
    for i, (_, _, kt, use) in enumerate(units):
        peak = jnp.max(functools.reduce(jnp.maximum, peaks), axis=0, keepdims=True)
        sums, peaks = [], []
        ahead = []
        if i + 1 < len(units):
            ahead = score_steps(units[i + 1][0](), units[i + 1][1], scores[(i + 1) % 2], peaks)
        now = sum_steps(kt, scores[i % 2], peak, sums)
        for j in range(max(len(ahead), len(now))):
            for steps in (ahead, now):
                if j < len(steps):
                    steps[j]()
        total = functools.reduce(jnp.add, sums)
        row = lax.broadcasted_iota(jnp.int32, (8, CHUNK), 0)
        use(total[0:CH], jnp.where(row == 3, peak, total[CH:MSG]))


def merge(parts):
    peaks = [extra[3:4] for _, extra in parts]
    peak = functools.reduce(jnp.maximum, peaks)
    gains = [jnp.exp2((p - peak) * SCALE) for p in peaks]
    feat = sum(f * g for (f, _), g in zip(parts, gains))
    extra = sum(e * g for (_, e), g in zip(parts, gains))
    row = lax.broadcasted_iota(jnp.int32, extra.shape, 0)
    return feat, jnp.where(row == 3, peak, extra)


def pack(feat, extra, out):
    low_lane = lax.broadcasted_iota(jnp.int32, (PART, CH), 1) < PART
    low_extra = lax.broadcasted_iota(jnp.int32, (8, CH), 1) < PART
    for t in range(2):
        low, high = feat[0:PART, t * CH:(t + 1) * CH], feat[PART:CH, t * CH:(t + 1) * CH]
        ext = extra[:, t * CH:(t + 1) * CH]
        ext_roll = pltpu.roll(ext, PART, 1)
        out[2 * t, 0:PART] = jnp.where(low_lane, low, pltpu.roll(high, PART, 1))
        out[2 * t, PART:PACK] = jnp.where(low_extra, ext, ext_roll)
        out[2 * t + 1, 0:PART] = jnp.where(low_lane, pltpu.roll(low, PART, 1), high)
        out[2 * t + 1, PART:PACK] = jnp.where(low_extra, ext_roll, ext)


def finish(parts, first_pixel, warped, flow):
    feat, extra = merge(parts)
    inverse = 1.0 / extra[2:3]
    turned = (feat * inverse).T
    warped[:, 0:PART] = turned[0:PART]
    warped[:, PART:CH] = turned[PART:CH]
    pixel = first_pixel + lax.broadcasted_iota(jnp.int32, (1, PART), 1)
    column_pos, row_pos = grid_xy(pixel)
    coord = (extra * inverse)[:, 0:PART]
    flow[0:1] = coord[0:1] - column_pos
    flow[1:2] = coord[1:2] - row_pos


def kernel(
    f1_hbm, f2_hbm, warped_one, flow_one, warped_two, flow_two,
    f1, f2, kt_one, kt_two, scores_even, scores_odd,
    core_out, core_in, a1_out, a1_in, b1_out, b1_in, a2_out, a2_in, b2_out, b2_in,
    load, core_send, core_recv, a1_send, a1_recv, b1_send, b1_recv,
    a2_send, a2_recv, b2_send, b2_recv,
):
    load_one = pltpu.make_async_copy(f1_hbm, f1, load.at[0])
    load_two = pltpu.make_async_copy(f2_hbm, f2, load.at[1])
    load_one.start()
    load_two.start()

    aa, ba = lax.axis_index("aa"), lax.axis_index("ba")
    core = lax.rem(aa, 2)
    z = lax.rem(lax.div(aa, 2), 8)
    y_lo = lax.div(aa, 16)
    z_hi, z_lo = lax.div(z, 2), lax.rem(z, 2)
    x, y_hi = lax.div(ba, 4), lax.rem(ba, 4)

    def turn(value, offset):
        return lax.rem(value + offset, 4)

    def a1_peer(offset):
        return (aa, turn(x, offset) * 4 + y_hi)

    def a2_peer(offset):
        return (aa, x * 4 + turn(y_hi, offset))

    def b1_block(offset):
        return lax.rem(y_lo + offset // 2, 2) * 8 + lax.rem(z_lo + offset % 2, 2)

    def b1_peer(offset):
        return ((b1_block(offset) + z_hi * 2) * 2 + core, ba)

    def b2_peer(offset):
        return ((y_lo * 8 + turn(z_hi, offset) * 2 + z_lo) * 2 + core, ba)

    sibling = (aa + 1 - 2 * core, ba)

    def remote(src, dst, sems, slot, peer):
        return pltpu.make_async_remote_copy(
            src_ref=src, dst_ref=dst.at[slot], send_sem=sems[0].at[slot], recv_sem=sems[1].at[slot],
            device_id=peer, device_id_type=MESH,
        )

    core_copy = [
        remote(core_out.at[s], core_in, (core_send, core_recv), s, sibling) for s in range(4)
    ]
    a1_copy = {
        s: remote(a1_out.at[s], a1_in, (a1_send, a1_recv), s - 1, a1_peer(s)) for s in (1, 2, 3)
    }
    b1_copy = {
        s: remote(b1_out.at[s], b1_in, (b1_send, b1_recv), s - 1, b1_peer(s)) for s in (1, 2, 3)
    }
    a2_copy = {
        s: remote(a2_out.at[turn(y_hi, s)], a2_in, (a2_send, a2_recv), s - 1, a2_peer(s))
        for s in (1, 2, 3)
    }
    b2_copy = {
        s: remote(b2_out.at[turn(z_hi, s)], b2_in, (b2_send, b2_recv), s - 1, b2_peer(s))
        for s in (1, 2, 3)
    }

    barrier = pltpu.get_barrier_semaphore()
    for s in (2, 1, 3):
        for peers in (a2_peer, b2_peer, a1_peer, b1_peer):
            pl.semaphore_signal(barrier, inc=1, device_id=peers(s), device_id_type=MESH)
    pl.semaphore_signal(barrier, inc=1, device_id=sibling, device_id_type=MESH)

    load_one.wait()
    put_keys(kt_one, 0, f1[...], aa * f1.shape[0])
    load_two.wait()
    put_keys(kt_two, 0, f2[...], ba * f2.shape[0])

    def a_queries(offset):
        start = pl.multiple_of(turn(x, offset) * CHUNK, CHUNK)
        return f1[pl.ds(start, CHUNK)]

    def b_queries(offset, parity):
        blocks = []
        for j in range(4):
            start = pl.multiple_of(((b1_block(offset) + 2 * j) * 2 + parity) * PART, PART)
            blocks.append(f2[pl.ds(start, PART)])
        return jnp.concatenate(blocks, axis=0)

    def put(out):
        def use(feat, extra):
            out[0:CH] = feat
            out[CH:MSG] = extra

        return use

    def share(offset):
        core_copy[offset].wait_recv()
        mine, got = b1_out.at[offset], core_in.at[offset]
        feat, extra = merge([(mine[0:CH], mine[CH:MSG]), (got[0:CH], got[CH:MSG])])
        put(mine)(feat, extra)
        if offset:
            b1_copy[offset].start()

    def a_use(offset, shared):
        def use(feat, extra):
            if offset == A_ORDER[0]:
                pl.semaphore_wait(barrier, 13)
                for s in B_ORDER:
                    core_copy[s].start()
            put(a1_out.at[offset])(feat, extra)
            if offset:
                a1_copy[offset].start()
            for s in shared:
                share(s)

        return use

    units = [
        (functools.partial(b_queries, s, 1 - core), f1, kt_one, put(core_out.at[s])) for s in B_ORDER
    ]
    units += [
        (functools.partial(b_queries, s, core), f1, kt_one, put(b1_out.at[s])) for s in B_ORDER
    ]
    units += [
        (functools.partial(a_queries, s), f2, kt_two, a_use(s, shared))
        for s, shared in zip(A_ORDER, ((), B_ORDER[0:1], B_ORDER[1:3], B_ORDER[3:4]))
    ]
    attend(units, (scores_even, scores_odd))

    def first_merge(own, got, out):
        parts = [(own[0, 0:CH], own[0, CH:MSG])]
        parts += [(got[s, 0:CH], got[s, CH:MSG]) for s in range(3)]
        feat, extra = merge(parts)
        pack(feat, extra, out)

    def last_merge(mine, out, got, first_pixel, warped, flow):
        parts = [(out[mine, 0:PART], out[mine, PART:PACK])]
        parts += [(got[s, 0:PART], got[s, PART:PACK]) for s in range(3)]
        finish(parts, first_pixel, warped, flow)

    def wait_all(copies):
        for s in (1, 2, 3):
            copies[s].wait_recv()

    def start_all(copies):
        for s in (2, 1, 3):
            copies[s].start()

    wait_all(a1_copy)
    first_merge(a1_out, a1_in, a2_out)
    start_all(a2_copy)
    wait_all(b1_copy)
    first_merge(b1_out, b1_in, b2_out)
    start_all(b2_copy)
    wait_all(a2_copy)
    last_merge(y_hi, a2_out, a2_in, (aa * 16 + ba) * PART, warped_one, flow_one)
    wait_all(b2_copy)
    last_merge(z_hi, b2_out, b2_in, (ba * 32 + aa) * PART, warped_two, flow_two)

    for s in range(4):
        core_copy[s].wait_send()
    for copies in (a1_copy, b1_copy, a2_copy, b2_copy):
        for s in (1, 2, 3):
            copies[s].wait_send()


def emit(w1, g1, w2, g2, warped_one, flow_one, warped_two, flow_two, done):
    pairs = ((w1, warped_one), (g1, flow_one), (w2, warped_two), (g2, flow_two))
    copies = [pltpu.make_async_copy(src, dst, done.at[i]) for i, (src, dst) in enumerate(pairs)]
    for copy in copies:
        copy.start()
    for copy in copies:
        copy.wait()


def shards(frame_one, frame_two):
    rows_one, rows_two = frame_one.shape[0], frame_two.shape[0]
    vmem = pl.BlockSpec(memory_space=pltpu.VMEM)
    hbm = pl.BlockSpec(memory_space=pltpu.HBM)
    dma = pltpu.SemaphoreType.DMA
    shapes = (
        jax.ShapeDtypeStruct((PART, CH), F32),
        jax.ShapeDtypeStruct((2, PART), F32),
        jax.ShapeDtypeStruct((PART, CH), F32),
        jax.ShapeDtypeStruct((2, PART), F32),
    )
    results = pl.pallas_call(
        kernel,
        out_shape=shapes,
        in_specs=[hbm, hbm],
        out_specs=(vmem,) * 4,
        scratch_shapes=[
            pltpu.VMEM((rows_one, CH), BF16),
            pltpu.VMEM((rows_two, CH), BF16),
            pltpu.VMEM((AUG, rows_one), BF16),
            pltpu.VMEM((AUG, rows_two), BF16),
            pltpu.VMEM((rows_two, CHUNK), F32),
            pltpu.VMEM((rows_two, CHUNK), F32),
            pltpu.VMEM((4, MSG, CHUNK), F32),
            pltpu.VMEM((4, MSG, CHUNK), F32),
            pltpu.VMEM((4, MSG, CHUNK), F32),
            pltpu.VMEM((3, MSG, CHUNK), F32),
            pltpu.VMEM((4, MSG, CHUNK), F32),
            pltpu.VMEM((3, MSG, CHUNK), F32),
            pltpu.VMEM((4, PACK, CH), F32),
            pltpu.VMEM((3, PACK, CH), F32),
            pltpu.VMEM((4, PACK, CH), F32),
            pltpu.VMEM((3, PACK, CH), F32),
            dma((2,)),
            dma((4,)), dma((4,)),
            dma((3,)), dma((3,)), dma((3,)), dma((3,)),
            dma((3,)), dma((3,)), dma((3,)), dma((3,)),
        ],
        compiler_params=pltpu.CompilerParams(
            collective_id=0, has_side_effects=True, vmem_limit_bytes=54976 * 1024
        ),
        name="match",
    )(frame_one, frame_two)
    return pl.pallas_call(
        emit,
        out_shape=shapes,
        in_specs=[vmem] * 4,
        out_specs=(hbm,) * 4,
        scratch_shapes=[dma((4,))],
        compiler_params=pltpu.CompilerParams(vmem_limit_bytes=1024 * 1024),
        name="emit",
    )(*results)


def solution(mesh):
    return jax.shard_map(
        shards,
        mesh=mesh,
        in_specs=(P("aa", None), P("ba", None)),
        out_specs=(
            P(("aa", "ba"), None),
            P(None, ("aa", "ba")),
            P(("ba", "aa"), None),
            P(None, ("ba", "aa")),
        ),
        check_vma=False,
    )
```

time: 39.3 us -> 32.4 us (0.82)
  local copies, waits for them, and re-layouts: 4.34 us -> 0 us
  Pallas kernels: 34.1 us -> 31.6 us
    unnamed x8 -> x0, local copies, waits for them, and re-layouts: 4.34 us -> none
    pallas_call x1 -> x2, Pallas kernels: 34.1 us -> 31.6 us  [the longest x1 30.9 us: shards(): pl.pallas_call(kernel, out_shape=shapes, in_specs=[hbm, hbm], out_specs=(...]
where the time goes in v2:
time: 32.4 us; the launch traced here: 32.2 us
  Pallas kernels  31.6 us (98%)
  between operations  0.64 us (2%)
    pallas_call x1, Pallas kernels, shards(): pl.pallas_call(kernel, out_shape=shapes, in_specs=[hbm, hbm], out_specs=(...  30.9 us
    pallas_call x1, Pallas kernels, shards(): pl.pallas_call(emit, out_shape=shapes, in_specs=[vmem] * 4, out_specs=(hb...  0.67 us

profile of v2, /device:TPU:1, one launch (start us, length us, event | category | flops | bytes accessed | tf_op | source)
XLA Modules:
  0.0 32.2 jit_solution(15367363406340394023)
XLA Ops:
  0.6 30.9 %match.1 = (f32[64,128]{1,0:T(8,128)S(1)}, f32[2,64]{1,0:T(2,128)S(1)}, f32[64,128]{1,0:T(8,128)S(1)}, f32[2,64]{1,0:T(2,128)S(1)}) custom-call(bf16[1024,128]{1,0:T(8,128)(2,1)} %f1_hbm.1, bf16[2048,128]{1,0:T(8,128)(2,1)} %f2_hbm.1), custom_call_target="tpu_custom_call" | custom-call | tf_op jit(solution)/shard_map/match/pallas_call | solution.py:304
  31.6 0.7 %emit.1 = (f32[64,128]{1,0:T(8,128)}, f32[2,64]{1,0:T(2,128)}, f32[64,128]{1,0:T(8,128)}, f32[2,64]{1,0:T(2,128)}) custom-call(f32[64,128]{1,0:T(8,128)S(1)} %get-tuple-element.8.w1, f32[2,64]{1,0:T(2,128)S(1)} %get-tuple-element.9.g1, f32[64,128]{1,0:T(8,128)S(1)} %get-tuple-element.10.w2, f32[2,64]{1,0:T(2,128)S(1)} %get-tuple-element.11.g2), custom_call_target="tpu_custom_call" | custom-call | tf_op jit(solution)/shard_map/emit/pallas_call | solution.py:336

commit v3 on v2

v3 whole, which is shorter than its diff:
```python
import functools
import math

import jax
import jax.numpy as jnp
from jax import lax
from jax.experimental import pallas as pl
from jax.experimental.pallas import tpu as pltpu
from jax.sharding import PartitionSpec as P

IMG_W = 128
CH = 128
MSG = CH + 8
AUG = CH + 16
CHUNK = 256
PART = 64
PACK = PART + 8
TILE = 512
SCALE = CH ** (-0.5) * math.log2(math.e)
MESH = pl.DeviceIdType.MESH
Y_SLOTS = ((0, 1), (3, 2))
Z_SLOTS = ((0, 1), (2, 3))
F32 = jnp.float32
BF16 = jnp.bfloat16


def grid_xy(pixel):
    column_pos = lax.rem(pixel, IMG_W).astype(F32) / 64.0
    row_pos = lax.div(pixel, IMG_W).astype(F32) / 64.0
    return column_pos, row_pos


def put_keys(kt, start, keys, first_pixel):
    count = keys.shape[0]
    cols = pl.ds(start, count)
    kt[0:CH, cols] = keys.T
    row = lax.broadcasted_iota(jnp.int32, (16, count), 0)
    pixel = first_pixel + lax.broadcasted_iota(jnp.int32, (16, count), 1)
    column_pos, row_pos = grid_xy(pixel)
    extra = jnp.where(row == 0, column_pos, jnp.where(row == 1, row_pos, jnp.where(row == 2, 1.0, 0.0)))
    kt[CH:AUG, cols] = extra.astype(BF16)


def score_steps(queries, keys, scores, peaks):
    def step(first):
        rows = slice(first, first + TILE)
        tile = lax.dot_general(
            keys[rows], queries, (((1,), (1,)), ((), ())), preferred_element_type=F32
        )
        scores[rows] = tile
        peaks.append(jnp.max(tile.reshape(TILE // 8, 8, CHUNK), axis=0))

    return [functools.partial(step, first) for first in range(0, keys.shape[0], TILE)]


def sum_steps(kt, scores, peak, sums):
    def step(first):
        cols = slice(first, first + TILE)
        weights = jnp.exp2((scores[cols] - peak) * SCALE).astype(BF16)
        sums.append(jnp.dot(kt[:, cols], weights, preferred_element_type=F32))

    return [functools.partial(step, first) for first in range(0, kt.shape[1], TILE)]


def attend(units, scores):
    peaks = []
    for step in score_steps(units[0][0](), units[0][1], scores[0], peaks):
        step()
    for i, (_, _, kt, use) in enumerate(units):
        peak = jnp.max(functools.reduce(jnp.maximum, peaks), axis=0, keepdims=True)
        sums, peaks = [], []
        ahead = []
        if i + 1 < len(units):
            ahead = score_steps(units[i + 1][0](), units[i + 1][1], scores[(i + 1) % 2], peaks)
        now = sum_steps(kt, scores[i % 2], peak, sums)
        for j in range(max(len(ahead), len(now))):
            for steps in (ahead, now):
                if j < len(steps):
                    steps[j]()
        total = functools.reduce(jnp.add, sums)
        row = lax.broadcasted_iota(jnp.int32, (8, CHUNK), 0)
        use(total[0:CH], jnp.where(row == 3, peak, total[CH:MSG]))


def merge(parts):
    peaks = [extra[3:4] for _, extra in parts]
    peak = functools.reduce(jnp.maximum, peaks)
    gains = [jnp.exp2((p - peak) * SCALE) for p in peaks]
    feat = sum(f * g for (f, _), g in zip(parts, gains))
    extra = sum(e * g for (_, e), g in zip(parts, gains))
    row = lax.broadcasted_iota(jnp.int32, extra.shape, 0)
    return feat, jnp.where(row == 3, peak, extra)


def pack(feat, extra, out, slots):
    low_lane = lax.broadcasted_iota(jnp.int32, (PART, CH), 1) < PART
    low_extra = lax.broadcasted_iota(jnp.int32, (8, CH), 1) < PART
    low, high = feat[0:PART], feat[PART:CH]
    turned = pltpu.roll(extra, PART, 1)
    out[slots[0], 0:PART] = jnp.where(low_lane, low, pltpu.roll(high, PART, 1))
    out[slots[0], PART:PACK] = jnp.where(low_extra, extra, turned)
    out[slots[1], 0:PART] = jnp.where(low_lane, pltpu.roll(low, PART, 1), high)
    out[slots[1], PART:PACK] = jnp.where(low_extra, turned, extra)


def finish(parts, first_pixel, warped, flow):
    feat, extra = merge(parts)
    inverse = 1.0 / extra[2:3]
    turned = (feat * inverse).T
    warped[:, 0:PART] = turned[0:PART]
    warped[:, PART:CH] = turned[PART:CH]
    pixel = first_pixel + lax.broadcasted_iota(jnp.int32, (1, PART), 1)
    column_pos, row_pos = grid_xy(pixel)
    coord = (extra * inverse)[:, 0:PART]
    flow[0:1] = coord[0:1] - column_pos
    flow[1:2] = coord[1:2] - row_pos


class Group:
    def __init__(self, rank, peer, out, got, sems):
        self.rank, self.peer, self.out, self.got = rank, peer, out, got
        self.send_sem, self.recv_sem = sems

    def others(self):
        return [lax.rem(self.rank + t, 4) for t in range(1, 4)]

    def greet(self, barrier):
        for k in self.others():
            pl.semaphore_signal(barrier, inc=1, device_id=self.peer(k), device_id_type=MESH)

    def copy(self, k, half=0):
        to, mine = 4 * half + k, 4 * half + self.rank
        return pltpu.make_async_remote_copy(
            src_ref=self.out.at[to], dst_ref=self.got.at[mine],
            send_sem=self.send_sem.at[to], recv_sem=self.recv_sem.at[mine],
            device_id=self.peer(k), device_id_type=MESH,
        )

    def send(self, k, half=0):
        @pl.when(k != self.rank)
        def _():
            self.copy(k, half).start()

    def wait_recv(self, half=0):
        for k in self.others():
            slot = 4 * half + k
            pltpu.make_async_remote_copy(
                src_ref=self.out.at[slot], dst_ref=self.got.at[slot],
                send_sem=self.send_sem.at[slot], recv_sem=self.recv_sem.at[slot],
                device_id=self.peer(k), device_id_type=MESH,
            ).wait_recv()

    def wait_send(self, half=0):
        for k in self.others():
            self.copy(k, half).wait_send()

    def parts(self, rows, half=0):
        own = self.out.at[4 * half + self.rank]
        parts = [(own[0:rows], own[rows:rows + 8])]
        for k in self.others():
            got = self.got.at[4 * half + k]
            parts.append((got[0:rows], got[rows:rows + 8]))
        return parts


class RankedGroup(Group):
    def __init__(self, rank, peer, out, got, sems):
        super().__init__(rank, peer, out, got, sems[0:2])
        self.ready = sems[2]

    def greet(self, barrier):
        for k in range(4):
            @pl.when(k > self.rank)
            def _():
                pl.semaphore_signal(barrier, inc=1, device_id=self.peer(k), device_id_type=MESH)

    def answer(self):
        for k in range(4):
            @pl.when(k < self.rank)
            def _():
                pl.semaphore_signal(
                    self.ready.at[self.rank], inc=1, device_id=self.peer(k), device_id_type=MESH
                )

    def send(self, k, half=0):
        @pl.when(k < self.rank)
        def _():
            self.copy(k).start()

        @pl.when(k > self.rank)
        def _():
            pl.semaphore_wait(self.ready.at[k], 1)
            self.copy(k).start()


def kernel(
    f1_hbm, f2_hbm, warped_one, flow_one, warped_two, flow_two,
    f1, f2, kt_one, kt_two, scores_even, scores_odd,
    core_out, core_in, core_own, x_out, x_in, w_out, w_in, y_out, y_in, z_out, z_in,
    load, core_send, core_recv, x_send, x_recv, w_send, w_recv, y_send, y_recv, z_send, z_recv,
    y_ready, z_ready,
):
    load_one = pltpu.make_async_copy(f1_hbm, f1, load.at[0])
    load_two = pltpu.make_async_copy(f2_hbm, f2, load.at[1])
    load_one.start()
    load_two.start()

    aa, ba = lax.axis_index("aa"), lax.axis_index("ba")
    core = lax.rem(aa, 2)
    z = lax.rem(lax.div(aa, 2), 8)
    y_lo = lax.div(aa, 16)
    z_hi, z_lo = lax.div(z, 2), lax.rem(z, 2)
    x, y_hi = lax.div(ba, 4), lax.rem(ba, 4)

    def y_slot(value):
        return value + lax.div(value, 2) * (5 - 2 * value)

    sibling = (aa + 1 - 2 * core, ba)
    x_group = Group(x, lambda k: (aa, k * 4 + y_hi), x_out, x_in, (x_send, x_recv))
    w_group = Group(
        y_lo * 2 + z_lo,
        lambda k: ((lax.div(k, 2) * 8 + z_hi * 2 + lax.rem(k, 2)) * 2 + core, ba),
        w_out, w_in, (w_send, w_recv),
    )
    y_group = RankedGroup(
        y_slot(y_hi), lambda k: (aa, x * 4 + y_slot(k)), y_out, y_in, (y_send, y_recv, y_ready)
    )
    z_group = RankedGroup(
        z_hi, lambda k: ((y_lo * 8 + k * 2 + z_lo) * 2 + core, ba), z_out, z_in, (z_send, z_recv, z_ready)
    )

    barrier = pltpu.get_barrier_semaphore()
    pl.semaphore_signal(barrier, inc=1, device_id=sibling, device_id_type=MESH)
    for group in (w_group, x_group, z_group, y_group):
        group.greet(barrier)

    load_one.wait()
    put_keys(kt_one, 0, f1[...], aa * f1.shape[0])
    load_two.wait()

    core_copy = [
        pltpu.make_async_remote_copy(
            src_ref=core_out.at[u], dst_ref=core_in.at[u],
            send_sem=core_send.at[u], recv_sem=core_recv.at[u],
            device_id=sibling, device_id_type=MESH,
        )
        for u in range(4)
    ]

    def b_queries(half, pair, parity):
        blocks = []
        for k in (2 * pair, 2 * pair + 1):
            for j in (2 * half, 2 * half + 1):
                block = (k // 2) * 8 + 2 * j + k % 2
                start = pl.multiple_of((block * 2 + parity) * PART, PART)
                blocks.append(f2[pl.ds(start, PART)])
        return jnp.concatenate(blocks, axis=0)

    def a_queries(half, pair):
        starts = [k * CHUNK + half * CH for k in (2 * pair, 2 * pair + 1)]
        return jnp.concatenate([f1[start:start + CH] for start in starts], axis=0)

    def put(out, feat, extra):
        out[0:CH] = feat
        out[CH:MSG] = extra

    def split(out, half, pair, feat, extra):
        for t in range(2):
            lanes = slice(t * CH, (t + 1) * CH)
            put(out.at[4 * half + 2 * pair + t], feat[:, lanes], extra[:, lanes])

    def enter():
        pl.semaphore_wait(barrier, 7 + y_group.rank + z_group.rank)
        core_copy[0].start()
        core_copy[1].start()
        z_group.answer()
        y_group.answer()

    def share(half, pair):
        u = 2 * half + pair
        core_copy[u].wait_recv()
        mine, got = core_own.at[u], core_in.at[u]
        feat, extra = merge([(mine[0:CH], mine[CH:MSG]), (got[0:CH], got[CH:MSG])])
        split(w_out, half, pair, feat, extra)
        for k in (2 * pair, 2 * pair + 1):
            w_group.send(k, half)

    def second(first_group, second_group, half, slots):
        first_group.wait_recv(half)
        feat, extra = merge(first_group.parts(CH, half))
        pack(feat, extra, second_group.out, slots[half])
        for k in (2 * half, 2 * half + 1):
            second_group.send(k)

    def b_other(half, pair, after=()):
        def use(feat, extra):
            u = 2 * half + pair
            put(core_out.at[u], feat, extra)
            if half:
                core_copy[u].start()
            for step in after:
                step()

        return functools.partial(b_queries, half, pair, 1 - core), f1, kt_one, use

    def b_own(half, pair, after=()):
        def use(feat, extra):
            put(core_own.at[2 * half + pair], feat, extra)
            for step in after:
                step()

        return functools.partial(b_queries, half, pair, core), f1, kt_one, use

    def a_unit(half, pair, after=()):
        def use(feat, extra):
            split(x_out, half, pair, feat, extra)
            for k in (2 * pair, 2 * pair + 1):
                x_group.send(k, half)
            for step in after:
                step()

        return functools.partial(a_queries, half, pair), f2, kt_two, use

    def late_keys():
        put_keys(kt_two, 0, f2[...], ba * f2.shape[0])

    attend(
        [
            b_other(0, 0), b_other(0, 1, (enter,)), b_own(0, 0, (late_keys,)), b_own(0, 1),
            a_unit(0, 0, (lambda: share(0, 0), lambda: share(0, 1))), a_unit(0, 1),
            b_other(1, 0), b_other(1, 1), b_own(1, 0),
            b_own(1, 1, (lambda: second(w_group, z_group, 0, Z_SLOTS),)),
            a_unit(1, 0, (lambda: share(1, 0), lambda: share(1, 1))), a_unit(1, 1),
        ],
        (scores_even, scores_odd),
    )
    second(x_group, y_group, 0, Y_SLOTS)
    second(x_group, y_group, 1, Y_SLOTS)
    second(w_group, z_group, 1, Z_SLOTS)
    y_group.wait_recv()
    finish(y_group.parts(PART), (aa * 16 + ba) * PART, warped_one, flow_one)
    z_group.wait_recv()
    finish(z_group.parts(PART), (ba * 32 + aa) * PART, warped_two, flow_two)

    for u in range(4):
        core_copy[u].wait_send()
    for group in (x_group, w_group):
        group.wait_send(0)
        group.wait_send(1)
    y_group.wait_send()
    z_group.wait_send()


def emit(w1, g1, w2, g2, warped_one, flow_one, warped_two, flow_two, done):
    pairs = ((w1, warped_one), (g1, flow_one), (w2, warped_two), (g2, flow_two))
    copies = [pltpu.make_async_copy(src, dst, done.at[i]) for i, (src, dst) in enumerate(pairs)]
    for copy in copies:
        copy.start()
    for copy in copies:
        copy.wait()


def shards(frame_one, frame_two):
    rows_one, rows_two = frame_one.shape[0], frame_two.shape[0]
    vmem = pl.BlockSpec(memory_space=pltpu.VMEM)
    hbm = pl.BlockSpec(memory_space=pltpu.HBM)
    dma = pltpu.SemaphoreType.DMA
    shapes = (
        jax.ShapeDtypeStruct((PART, CH), F32),
        jax.ShapeDtypeStruct((2, PART), F32),
        jax.ShapeDtypeStruct((PART, CH), F32),
        jax.ShapeDtypeStruct((2, PART), F32),
    )
    results = pl.pallas_call(
        kernel,
        out_shape=shapes,
        in_specs=[hbm, hbm],
        out_specs=(vmem,) * 4,
        scratch_shapes=[
            pltpu.VMEM((rows_one, CH), BF16),
            pltpu.VMEM((rows_two, CH), BF16),
            pltpu.VMEM((AUG, rows_one), BF16),
            pltpu.VMEM((AUG, rows_two), BF16),
            pltpu.VMEM((rows_two, CHUNK), F32),
            pltpu.VMEM((rows_two, CHUNK), F32),
            pltpu.VMEM((4, MSG, CHUNK), F32),
            pltpu.VMEM((4, MSG, CHUNK), F32),
            pltpu.VMEM((4, MSG, CHUNK), F32),
            pltpu.VMEM((8, MSG, CH), F32),
            pltpu.VMEM((8, MSG, CH), F32),
            pltpu.VMEM((8, MSG, CH), F32),
            pltpu.VMEM((8, MSG, CH), F32),
            pltpu.VMEM((4, PACK, CH), F32),
            pltpu.VMEM((4, PACK, CH), F32),
            pltpu.VMEM((4, PACK, CH), F32),
            pltpu.VMEM((4, PACK, CH), F32),
            dma((2,)),
            dma((4,)), dma((4,)),
            dma((8,)), dma((8,)),
            dma((8,)), dma((8,)),
            dma((4,)), dma((4,)),
            dma((4,)), dma((4,)),
            pltpu.SemaphoreType.REGULAR((4,)),
            pltpu.SemaphoreType.REGULAR((4,)),
        ],
        compiler_params=pltpu.CompilerParams(
            collective_id=0, has_side_effects=True, vmem_limit_bytes=54976 * 1024
        ),
        name="match",
    )(frame_one, frame_two)
    return pl.pallas_call(
        emit,
        out_shape=shapes,
        in_specs=[vmem] * 4,
        out_specs=(hbm,) * 4,
        scratch_shapes=[dma((4,))],
        compiler_params=pltpu.CompilerParams(vmem_limit_bytes=1024 * 1024),
        name="emit",
    )(*results)


def solution(mesh):
    return jax.shard_map(
        shards,
        mesh=mesh,
        in_specs=(P("aa", None), P("ba", None)),
        out_specs=(
            P(("aa", "ba"), None),
            P(None, ("aa", "ba")),
            P(("ba", "aa"), None),
            P(None, ("ba", "aa")),
        ),
        check_vma=False,
    )
```

time: 32.4 us -> 26.7 us (0.82)
  the two profiles are of different devices: /device:TPU:1 before, /device:TPU:72 now
where the time goes in v3:
time: 26.7 us; the launch traced here: 26.6 us
  Pallas kernels  25.9 us (97%)
  between operations  0.64 us (2%)
    pallas_call x1, Pallas kernels, shards(): pl.pallas_call(kernel, out_shape=shapes, in_specs=[hbm, hbm], out_specs=(...  25.3 us
    pallas_call x1, Pallas kernels, shards(): pl.pallas_call(emit, out_shape=shapes, in_specs=[vmem] * 4, out_specs=(hb...  0.67 us

profile of v3, /device:TPU:72, one launch (start us, length us, event | category | flops | bytes accessed | tf_op | source)
XLA Modules:
  0.0 26.6 jit_solution(16976093905733760836)
XLA Ops:
  0.6 25.3 %match.1 = (f32[64,128]{1,0:T(8,128)S(1)}, f32[2,64]{1,0:T(2,128)S(1)}, f32[64,128]{1,0:T(8,128)S(1)}, f32[2,64]{1,0:T(2,128)S(1)}) custom-call(bf16[1024,128]{1,0:T(8,128)(2,1)} %f1_hbm.1, bf16[2048,128]{1,0:T(8,128)(2,1)} %f2_hbm.1), custom_call_target="tpu_custom_call" | custom-call | tf_op jit(solution)/shard_map/match/pallas_call | solution.py:374
  25.9 0.7 %emit.1 = (f32[64,128]{1,0:T(8,128)}, f32[2,64]{1,0:T(2,128)}, f32[64,128]{1,0:T(8,128)}, f32[2,64]{1,0:T(2,128)}) custom-call(f32[64,128]{1,0:T(8,128)S(1)} %get-tuple-element.8.w1, f32[2,64]{1,0:T(2,128)S(1)} %get-tuple-element.9.g1, f32[64,128]{1,0:T(8,128)S(1)} %get-tuple-element.10.w2, f32[2,64]{1,0:T(2,128)S(1)} %get-tuple-element.11.g2), custom_call_target="tpu_custom_call" | custom-call | tf_op jit(solution)/shard_map/emit/pallas_call | solution.py:411

commit v4 on v3

--- a/solution.py
+++ b/solution.py
@@ -18,8 +18,7 @@
 TILE = 512
 SCALE = CH ** (-0.5) * math.log2(math.e)
 MESH = pl.DeviceIdType.MESH
-Y_SLOTS = ((0, 1), (3, 2))
-Z_SLOTS = ((0, 1), (2, 3))
+Y_ORDER = (0, 1, 3, 2)
 F32 = jnp.float32
 BF16 = jnp.bfloat16
 
@@ -73,10 +72,8 @@
         if i + 1 < len(units):
             ahead = score_steps(units[i + 1][0](), units[i + 1][1], scores[(i + 1) % 2], peaks)
         now = sum_steps(kt, scores[i % 2], peak, sums)
-        for j in range(max(len(ahead), len(now))):
-            for steps in (ahead, now):
-                if j < len(steps):
-                    steps[j]()
+        for step in ahead + now:
+            step()
         total = functools.reduce(jnp.add, sums)
         row = lax.broadcasted_iota(jnp.int32, (8, CHUNK), 0)
         use(total[0:CH], jnp.where(row == 3, peak, total[CH:MSG]))
@@ -92,15 +89,18 @@
     return feat, jnp.where(row == 3, peak, extra)
 
 
-def pack(feat, extra, out, slots):
+def pack(feat, extra, out, first):
     low_lane = lax.broadcasted_iota(jnp.int32, (PART, CH), 1) < PART
     low_extra = lax.broadcasted_iota(jnp.int32, (8, CH), 1) < PART
-    low, high = feat[0:PART], feat[PART:CH]
-    turned = pltpu.roll(extra, PART, 1)
-    out[slots[0], 0:PART] = jnp.where(low_lane, low, pltpu.roll(high, PART, 1))
-    out[slots[0], PART:PACK] = jnp.where(low_extra, extra, turned)
-    out[slots[1], 0:PART] = jnp.where(low_lane, pltpu.roll(low, PART, 1), high)
-    out[slots[1], PART:PACK] = jnp.where(low_extra, turned, extra)
+    for t in range(2):
+        lanes = slice(t * CH, (t + 1) * CH)
+        low, high, ext = feat[0:PART, lanes], feat[PART:CH, lanes], extra[:, lanes]
+        turned = pltpu.roll(ext, PART, 1)
+        even, odd = first + 2 * t, first + 2 * t + 1
+        out[even, 0:PART] = jnp.where(low_lane, low, pltpu.roll(high, PART, 1))
+        out[even, PART:PACK] = jnp.where(low_extra, ext, turned)
+        out[odd, 0:PART] = jnp.where(low_lane, pltpu.roll(low, PART, 1), high)
+        out[odd, PART:PACK] = jnp.where(low_extra, turned, ext)
 
 
 def finish(parts, first_pixel, warped, flow):
@@ -128,39 +128,34 @@
         for k in self.others():
             pl.semaphore_signal(barrier, inc=1, device_id=self.peer(k), device_id_type=MESH)
 
-    def copy(self, k, half=0):
-        to, mine = 4 * half + k, 4 * half + self.rank
+    def copy(self, k, e=0):
+        to, mine = 4 * e + k, 4 * e + self.rank
         return pltpu.make_async_remote_copy(
             src_ref=self.out.at[to], dst_ref=self.got.at[mine],
             send_sem=self.send_sem.at[to], recv_sem=self.recv_sem.at[mine],
             device_id=self.peer(k), device_id_type=MESH,
         )
 
-    def send(self, k, half=0):
-        @pl.when(k != self.rank)
-        def _():
-            self.copy(k, half).start()
-
-    def wait_recv(self, half=0):
+    def send(self, e):
         for k in self.others():
-            slot = 4 * half + k
+            self.copy(k, e).start()
+
+    def wait_recv(self, e=0):
+        for k in self.others():
+            slot = 4 * e + k
             pltpu.make_async_remote_copy(
                 src_ref=self.out.at[slot], dst_ref=self.got.at[slot],
                 send_sem=self.send_sem.at[slot], recv_sem=self.recv_sem.at[slot],
                 device_id=self.peer(k), device_id_type=MESH,
             ).wait_recv()
 
-    def wait_send(self, half=0):
+    def wait_send(self, e=0):
         for k in self.others():
-            self.copy(k, half).wait_send()
-
-    def parts(self, rows, half=0):
-        own = self.out.at[4 * half + self.rank]
-        parts = [(own[0:rows], own[rows:rows + 8])]
-        for k in self.others():
-            got = self.got.at[4 * half + k]
-            parts.append((got[0:rows], got[rows:rows + 8]))
-        return parts
+            self.copy(k, e).wait_send()
+
+    def parts(self, e=0):
+        blocks = [self.out.at[4 * e + self.rank]] + [self.got.at[4 * e + k] for k in self.others()]
+        return [(block[0:PART], block[PART:PACK]) for block in blocks]
 
 
 class RankedGroup(Group):
@@ -182,11 +177,12 @@
                     self.ready.at[self.rank], inc=1, device_id=self.peer(k), device_id_type=MESH
                 )
 
-    def send(self, k, half=0):
+    def send_lower(self, k):
         @pl.when(k < self.rank)
         def _():
             self.copy(k).start()
 
+    def send_higher(self, k):
         @pl.when(k > self.rank)
         def _():
             pl.semaphore_wait(self.ready.at[k], 1)
@@ -247,108 +243,106 @@
         for u in range(4)
     ]
 
-    def b_queries(half, pair, parity):
+    def b_queries(e, parity):
         blocks = []
-        for k in (2 * pair, 2 * pair + 1):
-            for j in (2 * half, 2 * half + 1):
-                block = (k // 2) * 8 + 2 * j + k % 2
-                start = pl.multiple_of((block * 2 + parity) * PART, PART)
-                blocks.append(f2[pl.ds(start, PART)])
+        for k in range(4):
+            block = (k // 2) * 8 + 2 * e + k % 2
+            start = pl.multiple_of((block * 2 + parity) * PART, PART)
+            blocks.append(f2[pl.ds(start, PART)])
         return jnp.concatenate(blocks, axis=0)
 
-    def a_queries(half, pair):
-        starts = [k * CHUNK + half * CH for k in (2 * pair, 2 * pair + 1)]
-        return jnp.concatenate([f1[start:start + CH] for start in starts], axis=0)
+    def a_queries(e):
+        starts = [k * CHUNK + Y_ORDER[e] * PART for k in range(4)]
+        return jnp.concatenate([f1[start:start + PART] for start in starts], axis=0)
 
     def put(out, feat, extra):
         out[0:CH] = feat
         out[CH:MSG] = extra
 
-    def split(out, half, pair, feat, extra):
-        for t in range(2):
-            lanes = slice(t * CH, (t + 1) * CH)
-            put(out.at[4 * half + 2 * pair + t], feat[:, lanes], extra[:, lanes])
-
     def enter():
         pl.semaphore_wait(barrier, 7 + y_group.rank + z_group.rank)
         core_copy[0].start()
-        core_copy[1].start()
         z_group.answer()
         y_group.answer()
 
-    def share(half, pair):
-        u = 2 * half + pair
-        core_copy[u].wait_recv()
-        mine, got = core_own.at[u], core_in.at[u]
+    def share(e):
+        core_copy[e].wait_recv()
+        mine, got = core_own.at[e], core_in.at[e]
         feat, extra = merge([(mine[0:CH], mine[CH:MSG]), (got[0:CH], got[CH:MSG])])
-        split(w_out, half, pair, feat, extra)
-        for k in (2 * pair, 2 * pair + 1):
-            w_group.send(k, half)
-
-    def second(first_group, second_group, half, slots):
-        first_group.wait_recv(half)
-        feat, extra = merge(first_group.parts(CH, half))
-        pack(feat, extra, second_group.out, slots[half])
-        for k in (2 * half, 2 * half + 1):
-            second_group.send(k)
-
-    def b_other(half, pair, after=()):
+        pack(feat, extra, w_out, 4 * e)
+        w_group.send(e)
+
+    def second(first_group, second_group, e):
+        first_group.wait_recv(e)
+        feat, extra = merge(first_group.parts(e))
+        second_group.out[e, 0:PART] = feat
+        second_group.out[e, PART:PACK] = extra
+        second_group.send_lower(e)
+
+    def b_other(e, *after):
         def use(feat, extra):
-            u = 2 * half + pair
-            put(core_out.at[u], feat, extra)
-            if half:
-                core_copy[u].start()
+            put(core_out.at[e], feat, extra)
+            if e:
+                core_copy[e].start()
             for step in after:
                 step()
 
-        return functools.partial(b_queries, half, pair, 1 - core), f1, kt_one, use
-
-    def b_own(half, pair, after=()):
+        return functools.partial(b_queries, e, 1 - core), f1, kt_one, use
+
+    def b_own(e, *after):
         def use(feat, extra):
-            put(core_own.at[2 * half + pair], feat, extra)
+            put(core_own.at[e], feat, extra)
             for step in after:
                 step()
 
-        return functools.partial(b_queries, half, pair, core), f1, kt_one, use
-
-    def a_unit(half, pair, after=()):
+        return functools.partial(b_queries, e, core), f1, kt_one, use
+
+    def a_unit(e, *after):
         def use(feat, extra):
-            split(x_out, half, pair, feat, extra)
-            for k in (2 * pair, 2 * pair + 1):
-                x_group.send(k, half)
+            pack(feat, extra, x_out, 4 * e)
+            x_group.send(e)
             for step in after:
                 step()
 
-        return functools.partial(a_queries, half, pair), f2, kt_two, use
+        return functools.partial(a_queries, e), f2, kt_two, use
 
     def late_keys():
         put_keys(kt_two, 0, f2[...], ba * f2.shape[0])
 
+    def do(step, *args):
+        return functools.partial(step, *args)
+
     attend(
         [
-            b_other(0, 0), b_other(0, 1, (enter,)), b_own(0, 0, (late_keys,)), b_own(0, 1),
-            a_unit(0, 0, (lambda: share(0, 0), lambda: share(0, 1))), a_unit(0, 1),
-            b_other(1, 0), b_other(1, 1), b_own(1, 0),
-            b_own(1, 1, (lambda: second(w_group, z_group, 0, Z_SLOTS),)),
-            a_unit(1, 0, (lambda: share(1, 0), lambda: share(1, 1))), a_unit(1, 1),
+            b_other(0), b_own(0, enter, late_keys), b_other(1), b_own(1), b_other(2, do(share, 0)),
+            a_unit(0, do(share, 1)), b_own(2), a_unit(1), b_other(3), b_own(3),
+            a_unit(2, do(second, w_group, z_group, 0), do(share, 2), do(share, 3)),
+            a_unit(3, do(second, w_group, z_group, 1)),
         ],
         (scores_even, scores_odd),
     )
-    second(x_group, y_group, 0, Y_SLOTS)
-    second(x_group, y_group, 1, Y_SLOTS)
-    second(w_group, z_group, 1, Z_SLOTS)
+    second(x_group, y_group, 0)
+    second(x_group, y_group, 1)
+    for k in range(2):
+        y_group.send_higher(k)
+    second(w_group, z_group, 2)
+    second(x_group, y_group, 2)
+    second(w_group, z_group, 3)
+    second(x_group, y_group, 3)
+    for k in range(2, 4):
+        y_group.send_higher(k)
+    for k in range(4):
+        z_group.send_higher(k)
     y_group.wait_recv()
-    finish(y_group.parts(PART), (aa * 16 + ba) * PART, warped_one, flow_one)
-    z_group.wait_recv()
-    finish(z_group.parts(PART), (ba * 32 + aa) * PART, warped_two, flow_two)
-
-    for u in range(4):
-        core_copy[u].wait_send()
-    for group in (x_group, w_group):
-        group.wait_send(0)
-        group.wait_send(1)
+    finish(y_group.parts(), (aa * 16 + ba) * PART, warped_one, flow_one)
+    for e in range(4):
+        core_copy[e].wait_send()
+        x_group.wait_send(e)
+        w_group.wait_send(e)
     y_group.wait_send()
     z_group.wait_send()
+    z_group.wait_recv()
+    finish(z_group.parts(), (ba * 32 + aa) * PART, warped_two, flow_two)
 
 
 def emit(w1, g1, w2, g2, warped_one, flow_one, warped_two, flow_two, done):
@@ -386,18 +380,18 @@
             pltpu.VMEM((4, MSG, CHUNK), F32),
             pltpu.VMEM((4, MSG, CHUNK), F32),
             pltpu.VMEM((4, MSG, CHUNK), F32),
-            pltpu.VMEM((8, MSG, CH), F32),
-            pltpu.VMEM((8, MSG, CH), F32),
-            pltpu.VMEM((8, MSG, CH), F32),
-            pltpu.VMEM((8, MSG, CH), F32),
+            pltpu.VMEM((16, PACK, CH), F32),
+            pltpu.VMEM((16, PACK, CH), F32),
+            pltpu.VMEM((16, PACK, CH), F32),
+            pltpu.VMEM((16, PACK, CH), F32),
             pltpu.VMEM((4, PACK, CH), F32),
             pltpu.VMEM((4, PACK, CH), F32),
             pltpu.VMEM((4, PACK, CH), F32),
             pltpu.VMEM((4, PACK, CH), F32),
             dma((2,)),
             dma((4,)), dma((4,)),
-            dma((8,)), dma((8,)),
-            dma((8,)), dma((8,)),
+            dma((16,)), dma((16,)),
+            dma((16,)), dma((16,)),
             dma((4,)), dma((4,)),
             dma((4,)), dma((4,)),
             pltpu.SemaphoreType.REGULAR((4,)),

time: 26.7 us -> 25.9 us (0.970)
  the two profiles are of different devices: /device:TPU:72 before, /device:TPU:144 now
where the time goes in v4:
time: 25.9 us; the launch traced here: 25.7 us
  Pallas kernels  25.1 us (97%)
  between operations  0.64 us (2%)
    pallas_call x1, Pallas kernels, shards(): pl.pallas_call(kernel, out_shape=shapes, in_specs=[hbm, hbm], out_specs=(...  24.4 us
    pallas_call x1, Pallas kernels, shards(): pl.pallas_call(emit, out_shape=shapes, in_specs=[vmem] * 4, out_specs=(hb...  0.67 us

profile of v4, /device:TPU:144, one launch (start us, length us, event | category | flops | bytes accessed | tf_op | source)
XLA Modules:
  0.0 25.7 jit_solution(15707565660386325950)
XLA Ops:
  0.6 24.4 %match.1 = (f32[64,128]{1,0:T(8,128)S(1)}, f32[2,64]{1,0:T(2,128)S(1)}, f32[64,128]{1,0:T(8,128)S(1)}, f32[2,64]{1,0:T(2,128)S(1)}) custom-call(bf16[1024,128]{1,0:T(8,128)(2,1)} %f1_hbm.1, bf16[2048,128]{1,0:T(8,128)(2,1)} %f2_hbm.1), custom_call_target="tpu_custom_call" | custom-call | tf_op jit(solution)/shard_map/match/pallas_call | solution.py:368
  25.1 0.7 %emit.1 = (f32[64,128]{1,0:T(8,128)}, f32[2,64]{1,0:T(2,128)}, f32[64,128]{1,0:T(8,128)}, f32[2,64]{1,0:T(2,128)}) custom-call(f32[64,128]{1,0:T(8,128)S(1)} %get-tuple-element.8.w1, f32[2,64]{1,0:T(2,128)S(1)} %get-tuple-element.9.g1, f32[64,128]{1,0:T(8,128)S(1)} %get-tuple-element.10.w2, f32[2,64]{1,0:T(2,128)S(1)} %get-tuple-element.11.g2), custom_call_target="tpu_custom_call" | custom-call | tf_op jit(solution)/shard_map/emit/pallas_call | solution.py:405

commit v5 on v4

--- a/solution.py
+++ b/solution.py
@@ -10,11 +10,12 @@
 
 IMG_W = 128
 CH = 128
-MSG = CH + 8
+EXTRA = 4
+MSG = CH + EXTRA
 AUG = CH + 16
 CHUNK = 256
 PART = 64
-PACK = PART + 8
+PACK = PART + EXTRA
 TILE = 512
 SCALE = CH ** (-0.5) * math.log2(math.e)
 MESH = pl.DeviceIdType.MESH
@@ -75,7 +76,7 @@
         for step in ahead + now:
             step()
         total = functools.reduce(jnp.add, sums)
-        row = lax.broadcasted_iota(jnp.int32, (8, CHUNK), 0)
+        row = lax.broadcasted_iota(jnp.int32, (EXTRA, CHUNK), 0)
         use(total[0:CH], jnp.where(row == 3, peak, total[CH:MSG]))
 
 
@@ -91,7 +92,7 @@
 
 def pack(feat, extra, out, first):
     low_lane = lax.broadcasted_iota(jnp.int32, (PART, CH), 1) < PART
-    low_extra = lax.broadcasted_iota(jnp.int32, (8, CH), 1) < PART
+    low_extra = lax.broadcasted_iota(jnp.int32, (EXTRA, CH), 1) < PART
     for t in range(2):
         lanes = slice(t * CH, (t + 1) * CH)
         low, high, ext = feat[0:PART, lanes], feat[PART:CH, lanes], extra[:, lanes]
@@ -117,16 +118,31 @@
 
 
 class Group:
-    def __init__(self, rank, peer, out, got, sems):
-        self.rank, self.peer, self.out, self.got = rank, peer, out, got
-        self.send_sem, self.recv_sem = sems
+    def __init__(self, rank, peer, out, got, sems, span=1):
+        self.rank, self.peer, self.out, self.got, self.span = rank, peer, out, got, span
+        self.send_sem, self.recv_sem, self.ready = sems
+        self.level = lax.div(rank, span)
+        self.greeted = self.level * span + span - 1
 
     def others(self):
         return [lax.rem(self.rank + t, 4) for t in range(1, 4)]
 
     def greet(self, barrier):
-        for k in self.others():
-            pl.semaphore_signal(barrier, inc=1, device_id=self.peer(k), device_id_type=MESH)
+        for k in range(4):
+            @pl.when((k // self.span >= self.level) & (k != self.rank))
+            def _():
+                pl.semaphore_signal(barrier, inc=1, device_id=self.peer(k), device_id_type=MESH)
+
+    def answer(self):
+        for k in range(4 - self.span):
+            @pl.when(k // self.span < self.level)
+            def _():
+                pl.semaphore_signal(
+                    self.ready.at[self.rank], inc=1, device_id=self.peer(k), device_id_type=MESH
+                )
+
+    def wait_ready(self, k):
+        pl.semaphore_wait(self.ready.at[k], 1)
 
     def copy(self, k, e=0):
         to, mine = 4 * e + k, 4 * e + self.rank
@@ -136,9 +152,28 @@
             device_id=self.peer(k), device_id_type=MESH,
         )
 
+    def send_lower(self, k, e=0):
+        @pl.when((k // self.span <= self.level) & (k != self.rank))
+        def _():
+            self.copy(k, e).start()
+
+    def send_higher(self, k, e=0):
+        @pl.when(k // self.span > self.level)
+        def _():
+            self.wait_ready(k)
+            self.copy(k, e).start()
+
     def send(self, e):
-        for k in self.others():
-            self.copy(k, e).start()
+        if e == 0:
+            for k in range(4):
+                self.send_lower(k)
+        else:
+            for k in self.others():
+                self.copy(k, e).start()
+
+    def send_first(self):
+        for k in range(self.span, 4):
+            self.send_higher(k)
 
     def wait_recv(self, e=0):
         for k in self.others():
@@ -158,43 +193,12 @@
         return [(block[0:PART], block[PART:PACK]) for block in blocks]
 
 
-class RankedGroup(Group):
-    def __init__(self, rank, peer, out, got, sems):
-        super().__init__(rank, peer, out, got, sems[0:2])
-        self.ready = sems[2]
-
-    def greet(self, barrier):
-        for k in range(4):
-            @pl.when(k > self.rank)
-            def _():
-                pl.semaphore_signal(barrier, inc=1, device_id=self.peer(k), device_id_type=MESH)
-
-    def answer(self):
-        for k in range(4):
-            @pl.when(k < self.rank)
-            def _():
-                pl.semaphore_signal(
-                    self.ready.at[self.rank], inc=1, device_id=self.peer(k), device_id_type=MESH
-                )
-
-    def send_lower(self, k):
-        @pl.when(k < self.rank)
-        def _():
-            self.copy(k).start()
-
-    def send_higher(self, k):
-        @pl.when(k > self.rank)
-        def _():
-            pl.semaphore_wait(self.ready.at[k], 1)
-            self.copy(k).start()
-
-
 def kernel(
     f1_hbm, f2_hbm, warped_one, flow_one, warped_two, flow_two,
     f1, f2, kt_one, kt_two, scores_even, scores_odd,
     core_out, core_in, core_own, x_out, x_in, w_out, w_in, y_out, y_in, z_out, z_in,
     load, core_send, core_recv, x_send, x_recv, w_send, w_recv, y_send, y_recv, z_send, z_recv,
-    y_ready, z_ready,
+    x_ready, w_ready, y_ready, z_ready,
 ):
     load_one = pltpu.make_async_copy(f1_hbm, f1, load.at[0])
     load_two = pltpu.make_async_copy(f2_hbm, f2, load.at[1])
@@ -212,22 +216,24 @@
         return value + lax.div(value, 2) * (5 - 2 * value)
 
     sibling = (aa + 1 - 2 * core, ba)
-    x_group = Group(x, lambda k: (aa, k * 4 + y_hi), x_out, x_in, (x_send, x_recv))
+    def w_peer(k):
+        return ((lax.rem(k, 2) * 8 + z_hi * 2 + lax.div(k, 2)) * 2 + core, ba)
+
+    x_group = Group(x, lambda k: (aa, k * 4 + y_hi), x_out, x_in, (x_send, x_recv, x_ready))
     w_group = Group(
-        y_lo * 2 + z_lo,
-        lambda k: ((lax.div(k, 2) * 8 + z_hi * 2 + lax.rem(k, 2)) * 2 + core, ba),
-        w_out, w_in, (w_send, w_recv),
-    )
-    y_group = RankedGroup(
+        z_lo * 2 + y_lo, w_peer, w_out, w_in, (w_send, w_recv, w_ready), 4
+    )
+    y_group = Group(
         y_slot(y_hi), lambda k: (aa, x * 4 + y_slot(k)), y_out, y_in, (y_send, y_recv, y_ready)
     )
-    z_group = RankedGroup(
+    z_group = Group(
         z_hi, lambda k: ((y_lo * 8 + k * 2 + z_lo) * 2 + core, ba), z_out, z_in, (z_send, z_recv, z_ready)
     )
 
     barrier = pltpu.get_barrier_semaphore()
     pl.semaphore_signal(barrier, inc=1, device_id=sibling, device_id_type=MESH)
-    for group in (w_group, x_group, z_group, y_group):
+    groups = (w_group, x_group, z_group, y_group)
+    for group in groups:
         group.greet(barrier)
 
     load_one.wait()
@@ -246,7 +252,7 @@
     def b_queries(e, parity):
         blocks = []
         for k in range(4):
-            block = (k // 2) * 8 + 2 * e + k % 2
+            block = (k % 2) * 8 + 2 * e + k // 2
             start = pl.multiple_of((block * 2 + parity) * PART, PART)
             blocks.append(f2[pl.ds(start, PART)])
         return jnp.concatenate(blocks, axis=0)
@@ -260,10 +266,10 @@
         out[CH:MSG] = extra
 
     def enter():
-        pl.semaphore_wait(barrier, 7 + y_group.rank + z_group.rank)
+        pl.semaphore_wait(barrier, 1 + sum(group.greeted for group in groups))
         core_copy[0].start()
-        z_group.answer()
-        y_group.answer()
+        for group in groups:
+            group.answer()
 
     def share(e):
         core_copy[e].wait_recv()
@@ -300,7 +306,8 @@
     def a_unit(e, *after):
         def use(feat, extra):
             pack(feat, extra, x_out, 4 * e)
-            x_group.send(e)
+            if e != 1:
+                x_group.send(e)
             for step in after:
                 step()
 
@@ -314,10 +321,11 @@
 
     attend(
         [
-            b_other(0), b_own(0, enter, late_keys), b_other(1), b_own(1), b_other(2, do(share, 0)),
-            a_unit(0, do(share, 1)), b_own(2), a_unit(1), b_other(3), b_own(3),
-            a_unit(2, do(second, w_group, z_group, 0), do(share, 2), do(share, 3)),
-            a_unit(3, do(second, w_group, z_group, 1)),
+            b_other(0, enter), b_own(0, late_keys), b_other(1), b_own(1), b_other(2, do(share, 0)),
+            a_unit(0, do(share, 1)), b_own(2), a_unit(1), b_other(3),
+            b_own(3, x_group.send_first, do(x_group.send, 1)),
+            a_unit(2, do(second, w_group, z_group, 0), do(share, 2)),
+            a_unit(3, do(second, w_group, z_group, 1), do(share, 3)),
         ],
         (scores_even, scores_odd),
     )
@@ -325,12 +333,12 @@
     second(x_group, y_group, 1)
     for k in range(2):
         y_group.send_higher(k)
-    second(w_group, z_group, 2)
     second(x_group, y_group, 2)
-    second(w_group, z_group, 3)
     second(x_group, y_group, 3)
     for k in range(2, 4):
         y_group.send_higher(k)
+    second(w_group, z_group, 2)
+    second(w_group, z_group, 3)
     for k in range(4):
         z_group.send_higher(k)
     y_group.wait_recv()
@@ -339,10 +347,10 @@
         core_copy[e].wait_send()
         x_group.wait_send(e)
         w_group.wait_send(e)
+    z_group.wait_recv()
+    finish(z_group.parts(), (ba * 32 + aa) * PART, warped_two, flow_two)
     y_group.wait_send()
     z_group.wait_send()
-    z_group.wait_recv()
-    finish(z_group.parts(), (ba * 32 + aa) * PART, warped_two, flow_two)
 
 
 def emit(w1, g1, w2, g2, warped_one, flow_one, warped_two, flow_two, done):
@@ -396,6 +404,8 @@
             dma((4,)), dma((4,)),
             pltpu.SemaphoreType.REGULAR((4,)),
             pltpu.SemaphoreType.REGULAR((4,)),
+            pltpu.SemaphoreType.REGULAR((4,)),
+            pltpu.SemaphoreType.REGULAR((4,)),
         ],
         compiler_params=pltpu.CompilerParams(
             collective_id=0, has_side_effects=True, vmem_limit_bytes=54976 * 1024

time: 25.9 us -> 25.3 us (0.977)
  the two profiles are of different devices: /device:TPU:144 before, /device:TPU:6 now
where the time goes in v5:
time: 25.3 us; the launch traced here: 25.2 us
  Pallas kernels  24.5 us (97%)
  between operations  0.64 us (3%)
    pallas_call x1, Pallas kernels, shards(): pl.pallas_call(kernel, out_shape=shapes, in_specs=[hbm, hbm], out_specs=(...  23.8 us
    pallas_call x1, Pallas kernels, shards(): pl.pallas_call(emit, out_shape=shapes, in_specs=[vmem] * 4, out_specs=(hb...  0.67 us

profile of v5, /device:TPU:6, one launch (start us, length us, event | category | flops | bytes accessed | tf_op | source)
XLA Modules:
  0.0 25.2 jit_solution(8592893734254042660)
XLA Ops:
  0.6 23.8 %match.1 = (f32[64,128]{1,0:T(8,128)S(1)}, f32[2,64]{1,0:T(2,128)S(1)}, f32[64,128]{1,0:T(8,128)S(1)}, f32[2,64]{1,0:T(2,128)S(1)}) custom-call(bf16[1024,128]{1,0:T(8,128)(2,1)} %f1_hbm.1, bf16[2048,128]{1,0:T(8,128)(2,1)} %f2_hbm.1), custom_call_target="tpu_custom_call" | custom-call | tf_op jit(solution)/shard_map/match/pallas_call | solution.py:376
  24.5 0.7 %emit.1 = (f32[64,128]{1,0:T(8,128)}, f32[2,64]{1,0:T(2,128)}, f32[64,128]{1,0:T(8,128)}, f32[2,64]{1,0:T(2,128)}) custom-call(f32[64,128]{1,0:T(8,128)S(1)} %get-tuple-element.8.w1, f32[2,64]{1,0:T(2,128)S(1)} %get-tuple-element.9.g1, f32[64,128]{1,0:T(8,128)S(1)} %get-tuple-element.10.w2, f32[2,64]{1,0:T(2,128)S(1)} %get-tuple-element.11.g2), custom_call_target="tpu_custom_call" | custom-call | tf_op jit(solution)/shard_map/emit/pallas_call | solution.py:415

commit v6 on v5

--- a/solution.py
+++ b/solution.py
@@ -322,7 +322,7 @@
     attend(
         [
             b_other(0, enter), b_own(0, late_keys), b_other(1), b_own(1), b_other(2, do(share, 0)),
-            a_unit(0, do(share, 1)), b_own(2), a_unit(1), b_other(3),
+            a_unit(0), b_own(2, do(share, 1)), a_unit(1), b_other(3),
             b_own(3, x_group.send_first, do(x_group.send, 1)),
             a_unit(2, do(second, w_group, z_group, 0), do(share, 2)),
             a_unit(3, do(second, w_group, z_group, 1), do(share, 3)),

time: 25.3 us -> 25.5 us (level)
  no operation moved by 1% of the time
where the time goes in v6:
time: 25.5 us; the launch traced here: 25.3 us
  Pallas kernels  24.7 us (97%)
  between operations  0.64 us (3%)
    pallas_call x1, Pallas kernels, shards(): pl.pallas_call(kernel, out_shape=shapes, in_specs=[hbm, hbm], out_specs=(...  24 us
    pallas_call x1, Pallas kernels, shards(): pl.pallas_call(emit, out_shape=shapes, in_specs=[vmem] * 4, out_specs=(hb...  0.67 us

profile of v6, /device:TPU:6, one launch (start us, length us, event | category | flops | bytes accessed | tf_op | source)
XLA Modules:
  0.0 25.3 jit_solution(3470339050484879342)
XLA Ops:
  0.6 24.0 %match.1 = (f32[64,128]{1,0:T(8,128)S(1)}, f32[2,64]{1,0:T(2,128)S(1)}, f32[64,128]{1,0:T(8,128)S(1)}, f32[2,64]{1,0:T(2,128)S(1)}) custom-call(bf16[1024,128]{1,0:T(8,128)(2,1)} %f1_hbm.1, bf16[2048,128]{1,0:T(8,128)(2,1)} %f2_hbm.1), custom_call_target="tpu_custom_call" | custom-call | tf_op jit(solution)/shard_map/match/pallas_call | solution.py:376
  24.6 0.7 %emit.1 = (f32[64,128]{1,0:T(8,128)}, f32[2,64]{1,0:T(2,128)}, f32[64,128]{1,0:T(8,128)}, f32[2,64]{1,0:T(2,128)}) custom-call(f32[64,128]{1,0:T(8,128)S(1)} %get-tuple-element.8.w1, f32[2,64]{1,0:T(2,128)S(1)} %get-tuple-element.9.g1, f32[64,128]{1,0:T(8,128)S(1)} %get-tuple-element.10.w2, f32[2,64]{1,0:T(2,128)S(1)} %get-tuple-element.11.g2), custom_call_target="tpu_custom_call" | custom-call | tf_op jit(solution)/shard_map/emit/pallas_call | solution.py:415
